TPU v7x, 512 devices: a whole 4x4x16 slice. The times are simulated.
512 devices in a mesh: row: 128 (over z, y, x_hi), head: 4 (over x_lo, core).
Axes of the slice: x: 4 (x_hi: 2, x_lo: 2; x = x_hi * 2 + x_lo), y: 4, z: 16, core: 2. Of those that a mesh axis runs over, the one named last changes fastest.
Arguments:
- pair_rep: float32 [512, 512, 128], P('row'), may hold values from -6 to 6
- residue_mask: int32 [512], replicated, may hold values 0 or 1
- chain_ids: int32 [512], replicated, may hold values from 0 to 5, never falling along the last dimension, each value on 1 to 170 neighbouring positions
- ln_gain: float32 [2, 128], replicated, may hold values from 0.5 to 1.5
- ln_shift: float32 [2, 128], replicated, may hold values from -4 to 4
- w_proj: float32 [2, 128, 4, 128], P(None, None, 'head'), may hold values from -0.5 to 0.5
- w_bias: float32 [2, 128, 4], P(None, None, 'head'), may hold values from -20 to 20
- chain_bias: float32 [2, 4], P(None, 'head'), may hold values from -2 to 2
- w_out: float32 [2, 128, 128], replicated, may hold values from -0.5 to 0.5
Outputs:
- paired: float32 [512, 512, 128], P(None, 'row')
Inputs may be any that keep to these rules, and one draw needn't show every extreme that they name: `chain_ids`: chain numbers never fall from one token to the next.
All inputs are finite; a program needn't handle non-finite values.
Results may differ from a plain program's by a relative error of at most 0.00035.
Values sent between devices are 32-bit elements; how exact they have to be, the bound alone decides.
A program may use at most 64 MiB of HBM per device.

v0:
```python
import math

import jax
import jax.numpy as jnp
from jax import lax
from jax.sharding import PartitionSpec as P

highest = lax.Precision.HIGHEST


def normalize(features, scale_gain, shift_row):
    average = jnp.mean(features, axis=-1, keepdims=True)
    centred = features - average
    spread = jnp.mean(centred * centred, axis=-1, keepdims=True)
    return centred * lax.rsqrt(spread + 1e-05) * scale_gain + shift_row


def shards(pair_rep, residue_mask, chain_ids, ln_gain, ln_shift, w_proj, w_bias, chain_bias, w_out):
    own_rows, token_count, channels = pair_rep.shape
    heads_here = w_proj.shape[2]
    head_size = w_proj.shape[3] // 4
    inverse_root = 1.0 / math.sqrt(head_size)
    key_bias = (residue_mask.astype(jnp.float32) - 1.0) * 1000000000.0
    normed = normalize(pair_rep, ln_gain[0], ln_shift[0])
    projected = jnp.einsum("rnc,che->rnhe", normed, w_proj[0], precision=highest)
    plane_rows = jnp.einsum("rnc,ch->hrn", normed, w_bias[0], precision=highest)
    queries = projected[..., :head_size] * inverse_root
    keys_all = projected[..., head_size : 2 * head_size]
    values_all = projected[..., 2 * head_size : 3 * head_size]
    gate_vals = jax.nn.sigmoid(projected[..., 3 * head_size :])
    plane_piece = lax.all_gather(plane_rows, "row", axis=1, tiled=True)
    block_len = plane_piece.shape[1]
    chains_block = chain_ids
    same_block = (chains_block[:, None] == chain_ids[None, :]).astype(jnp.float32)
    added_bias = (
        plane_piece + chain_bias[0][:, None, None] * same_block[None] + key_bias[None, None, :]
    )

    def one_row(operands):
        query_row, key_row, value_row, gate_row = operands
        scores = jnp.einsum("jhd,khd->hjk", query_row, key_row, precision=highest) + added_bias
        weights = jax.nn.softmax(scores, axis=-1)
        attended = jnp.einsum("hjk,khd->jhd", weights, value_row, precision=highest) * gate_row
        return attended.reshape(block_len, heads_here * head_size)

    attended = lax.map(one_row, (queries, keys_all, values_all, gate_vals))
    all_heads = lax.all_gather(attended, "head", axis=2, tiled=True)
    after_start = pair_rep + jnp.einsum("rne,ec->rnc", all_heads, w_out[0], precision=highest)
    columns = lax.all_to_all(after_start, "row", split_axis=1, concat_axis=0, tiled=True)
    normed_cols = normalize(columns, ln_gain[1], ln_shift[1])
    projected_cols = jnp.einsum("nrc,che->nrhe", normed_cols, w_proj[1], precision=highest)
    cols_major = jnp.transpose(projected_cols, (1, 0, 2, 3))
    queries_cols = cols_major[..., :head_size] * inverse_root
    keys_cols = cols_major[..., head_size : 2 * head_size]
    values_cols = cols_major[..., 2 * head_size : 3 * head_size]
    gates_cols = jax.nn.sigmoid(projected_cols[..., 3 * head_size :])
    plane_cols = jnp.einsum("nrc,ch->hnr", normed_cols, w_bias[1], precision=highest)
    plane_piece = lax.all_gather(plane_cols, "row", axis=2, tiled=True)
    query_block_len = plane_piece.shape[2]
    chains_block = chain_ids
    same_block = (chains_block[:, None] == chain_ids[None, :]).astype(jnp.float32)
    query_added_bias = (
        jnp.transpose(plane_piece, (0, 2, 1))
        + chain_bias[1][:, None, None] * same_block[None]
        + key_bias[None, None, :]
    )

    def one_column(operands):
        query_col, key_col, value_col = operands
        scores = (
            jnp.einsum("ihd,khd->hik", query_col, key_col, precision=highest) + query_added_bias
        )
        weights = jax.nn.softmax(scores, axis=-1)
        return jnp.einsum("hik,khd->ihd", weights, value_col, precision=highest)

    result = lax.map(one_column, (queries_cols, keys_cols, values_cols))
    result = jnp.transpose(result, (1, 0, 2, 3)) * gates_cols
    ending = result.reshape(query_block_len, own_rows, heads_here * head_size)
    end_all = lax.all_gather(ending, "head", axis=2, tiled=True)
    return columns + jnp.einsum("nre,ec->nrc", end_all, w_out[1], precision=highest)


def solution(mesh):
    in_specs = (
        P("row", None, None),
        P(),
        P(),
        P(),
        P(),
        P(None, None, "head", None),
        P(None, None, "head"),
        P(None, "head"),
        P(),
    )
    out_specs = P(None, "row", None)
    return jax.shard_map(shards, mesh=mesh, in_specs=in_specs, out_specs=out_specs, check_vma=False)
```

profile of v0, /device:TPU:1, one launch (start us, length us, event | category | flops | bytes accessed | tf_op | source)
XLA Modules:
  0.0 585.1 jit_solution(1857927041730259705)
XLA Ops:
  6.5 1.7 reduce_sum.54
  8.2 0.6 multiply_reduce_fusion.1
  8.9 0.6 copy-done.7
  9.6 0.7 copy-done.9
  10.3 1.6 fusion.33
  11.8 0.6 copy.56
  12.5 0.0 all-gather.10.cloned.1.call-start
  12.5 0.6 copy-done.6
  13.2 0.6 fusion.63
  13.8 1.9 convolution_bitcast_fusion.2
  15.7 0.9 fusion.49
  16.7 186.6 %all-gather.14.cloned.1.call-done = f32[128,4,512]{2,1,0:T(4,128)} async-done(((f32[1,4,512]{2,1,0:T(4,128)}), f32[128,4,512]{2,1,0:T(4,128)}) %all-gather.14.cloned.1.call-update) | async-done | bytes 1048592 | tf_op jit(solution)/shard_map/all_gather | solution.py:31
  203.3 1.6 reshape.238
  204.9 0.7 copy-done.4
  205.6 0.9 fusion.29
  206.5 0.3 copy.44
  206.8 17.7 %while.20 = (s32[]{:T(128)}, f32[4,512,32]{1,2,0:T(8,128)}, f32[4,512,1,32]{1,3,0,2:T(8,128)}, f32[4,512,1,32]{1,3,0,2:T(8,128)}, f32[4,512,1,32]{1,3,0,2:T(8,12...) while((s32[]{:T(128)}, f32[4,512,32]{1,2,0:T(8,128)}, ...), condition=%wide.region_5.6_spmd, body=%wide.region_2.5_spmd.sunk | while | flops 202914816 | bytes 4534357 | solution.py:46
  206.8 1.9 fusion.83
  208.7 0.2 fusion.84
  208.9 2.3 fusion.85
  211.3 1.9 fusion.83
  213.1 0.2 fusion.84
  213.3 2.3 fusion.85
  215.7 1.9 fusion.83
  217.6 0.2 fusion.84
  217.8 2.3 fusion.85
  220.1 1.9 fusion.83
  222.0 0.2 fusion.84
  222.2 2.3 fusion.85
  224.6 0.0 all-gather.16.cloned.1.call-start
  224.6 32.9 %all-gather.10.cloned.1.call-done = f32[4,512,128]{1,2,0:T(8,128)} async-done(((f32[4,512,32]{1,2,0:T(8,128)}), f32[4,512,128]{1,2,0:T(8,128)}) %all-gather.10.cloned.1.call-update) | async-done | bytes 1048592 | tf_op jit(solution)/shard_map/all_gather | solution.py:47
  257.5 3.0 convolution_add_fusion.3
  260.5 0.7 copy.46
  261.2 68.0 %all_to_all.18 = f32[4,512,128]{2,0,1:T(4,128)S(1)} all-to-all(f32[4,512,128]{2,0,1:T(4,128)S(1)} %copy.46), channel_id=1, replica_groups=mesh['row'=128,'head'=4] {'row'}, dimensions={1} | all-to-all | bytes 2097152 | tf_op jit(solution)/shard_map/all_to_all | solution.py:49
  329.2 0.6 bitcast_reduce_fusion
  329.8 1.3 multiply_reduce_fusion
  331.2 1.4 multiply_add_fusion
  332.6 1.0 fusion.54
  333.5 0.9 copy.57
  334.5 0.0 all-gather.12.cloned.1.call-start
  334.5 1.1 fusion.64
  335.6 0.9 fusion.61
  336.5 180.2 %all-gather.16.cloned.1.call-done = f32[128,4,512]{2,1,0:T(4,128)} async-done(((f32[1,4,512]{2,1,0:T(4,128)}), f32[128,4,512]{2,1,0:T(4,128)}) %all-gather.16.cloned.1.call-update) | async-done | bytes 1048592 | tf_op jit(solution)/shard_map/all_gather | solution.py:58
  516.7 1.6 reshape.244
  518.3 1.8 fusion.31
  520.1 1.6 copy.52
  521.6 17.5 %while.21 = (s32[]{:T(128)}, f32[4,512,1,32]{1,3,2,0:T(8,128)}, f32[4,512,1,32]{1,3,0,2:T(8,128)}, f32[4,512,1,32]{1,3,0,2:T(8,128)}, f32[4,512,1,32]{1,3,0,2:T(...) while((s32[]{:T(128)}, f32[4,512,1,32]{1,3,2,0:T(8,128)}, f32[4,512,1,32]{1,3,0,2:T(8,128)}, ...), condition=%wide.region_11.12_spmd, body=%wide.region_8.11_spmd.sunk | while | flops 202898432 | bytes 4468813 | solution.py:76
  521.7 1.9 fusion.88
  523.6 0.2 fusion.89
  523.8 2.3 fusion.90
  526.0 1.9 fusion.88
  527.9 0.2 fusion.89
  528.1 2.3 fusion.90
  530.4 1.9 fusion.88
  532.3 0.2 fusion.89
  532.5 2.3 fusion.90
  534.8 1.9 fusion.88
  536.7 0.2 fusion.89
  536.9 2.3 fusion.90
  539.2 1.7 fusion.45
  540.9 0.2 copy.47
  541.1 32.7 %all-gather.12.cloned.1.call-done = f32[512,4,1,128]{0,3,1,2:T(8,128)} async-done(((f32[512,4,1,32]{0,3,1,2:T(8,128)}), f32[512,4,1,128]{0,3,1,2:T(8,128)}) %all-gather.12.cloned.1.call-update) | async-done | bytes 1048592 | tf_op jit(solution)/shard_map/all_gather | solution.py:79
  573.9 3.0 convolution_add_fusion.2
  576.9 1.6 copy.55
  (30 shorter events, 0.2 us)
Async XLA Ops:
  6.5 1.7 copy-start
  6.5 196.8 %all-gather.14.cloned.1.call-start = ((), (), s32[]{:S(2)}) async-start(), calls=%async_computation.3 | async-start | bytes 1056768 | tf_op jit(solution)/shard_map/all_gather | solution.py:31
  8.9 0.7 copy-start.7
  8.9 0.7 copy-start.8
  9.6 0.7 copy-start.9
  10.3 3.6 copy-start.3
  12.5 245.0 %all-gather.10.cloned.1.call-start = ((), (), s32[]{:S(2)}) async-start(), calls=%async_computation.1 | async-start | bytes 1310720 | tf_op jit(solution)/shard_map/all_gather | solution.py:47
  12.5 0.7 copy-start.6
  13.8 1.9 copy-start.5
  204.9 0.7 copy-start.4
  224.5 33.0 %copy-start.1 = (f32[2,128,128]{2,1,0:T(8,128)S(1)}, f32[2,128,128]{2,1,0:T(8,128)}, u32[]{:S(2)}) copy-start(f32[2,128,128]{2,1,0:T(8,128)} %param.21) | copy-start | bytes 393220
  224.6 292.2 %all-gather.16.cloned.1.call-start = ((), (), s32[]{:S(2)}) async-start(), calls=%async_computation.4 | async-start | bytes 1056768 | tf_op jit(solution)/shard_map/all_gather | solution.py:58
  334.5 239.4 %all-gather.12.cloned.1.call-start = ((), (), s32[]{:S(2)}) async-start(), calls=%async_computation.2 | async-start | bytes 1310720 | tf_op jit(solution)/shard_map/all_gather | solution.py:79
  540.9 32.9 %copy-start.2 = (f32[2,128,128]{2,1,0:T(8,128)S(1)}, f32[2,128,128]{2,1,0:T(8,128)}, u32[]{:S(2)}) copy-start(f32[2,128,128]{2,1,0:T(8,128)} %param.21) | copy-start | bytes 393220
Sparse Core Ops, SparseCore 0:
  12.6 190.6 all-gather.13
  224.7 32.7 all-gather.9
  334.6 182.0 all-gather.15
  541.0 32.7 all-gather.11
where the time goes:
time: 586 us; the launch traced here: 585 us
  waiting for transfers between devices  432 us (74%)
  blocking collectives  68 us (12%)
  matrix products  45.2 us (8%)
  other arithmetic  13.5 us (2%)
  between operations  13.4 us (2%)
  local copies, waits for them, and re-layouts  12.4 us (2%)
    all_gather x1, waiting for transfers between devices, shards(): plane_piece = lax.all_gather(plane_rows, 'row', axis=1, tiled=True)  187 us
    all_gather x1, waiting for transfers between devices, shards(): plane_piece = lax.all_gather(plane_cols, 'row', axis=2, tiled=True)  180 us
    all_to_all x1, blocking collectives, shards(): lax.all_to_all(after_start, 'row', split_axis=1, concat_axis=0, tiled=True)  68 us
    all_gather x1, waiting for transfers between devices, shards(): all_heads = lax.all_gather(attended, 'head', axis=2, tiled=True)  32.9 us
    all_gather x1, waiting for transfers between devices, shards(): end_all = lax.all_gather(ending, 'head', axis=2, tiled=True)  32.7 us
  transfers between devices with their start and end apart: 4, of which 4 were waited for; matrix products, arithmetic and copies ran while one was open for 1% of the time, Pallas kernels for 0%

commit v1 on v0

v1 whole, which is shorter than its diff:
```python
import functools
import math

import jax
import jax.numpy as jnp
from jax import lax
from jax.experimental import pallas as pl
from jax.experimental.pallas import tpu as pltpu
from jax.sharding import PartitionSpec as P

highest = lax.Precision.HIGHEST
MESH = pl.DeviceIdType.MESH
F32, BF16 = jnp.float32, jnp.bfloat16

GATHER = (0, 32)
PAIR_Z, PAIR_S = 64, 80
COL_CORE, COL_X, COL_FWD = 88, 96, 104
SMALL, W_CORE, W_X, W_FWD = 112, 116, 118, 120
OUT_CORE, OUT_X, OUT_FWD = 122, 126, 130
SLOTS = 134


def dot(a, b, dims, precision=None):
    return lax.dot_general(a, b, (dims, ((), ())), precision=precision, preferred_element_type=F32)


def split(x):
    high = x.astype(BF16)
    return high, (x - high.astype(F32)).astype(BF16)


def normalize(x, gain, shift):
    centred = x - jnp.mean(x, axis=-1, keepdims=True)
    spread = jnp.mean(centred * centred, axis=-1, keepdims=True)
    return centred * lax.rsqrt(spread + 1e-05) * gain + shift


def kernel(
    pair, mask, chain, ln_gain, ln_shift, w_own, wb_own, cb_own, w_out, out,
    xp, wp, small, plane0, plane1, after, mid, mid2, cols, k3, q3, vb, gates, bias, wall, marks, ss, rs,
):
    r, q = lax.axis_index("row"), lax.axis_index("head")
    z, s = r // 8, lax.rem(r, 8)
    y, xh = s // 2, lax.rem(s, 2)
    core, xlo = lax.rem(q, 2), q // 2
    other_core = (r, xlo * 2 + 1 - core)
    other_x = (r, (1 - xlo) * 2 + core)
    q_core, q_x = other_core[1], other_x[1]
    q_far = (1 - xlo) * 2 + 1 - core

    def at_z(k):
        return (lax.rem(z + k, 16) * 8 + s, q)

    def at_y(k):
        return (z * 8 + lax.rem(y + k, 4) * 2 + xh, q)

    def at_s(k):
        return (z * 8 + lax.rem(s + k, 8), q)

    at_x = (z * 8 + y * 2 + 1 - xh, q)

    def remote(src, dst, slot, device):
        return pltpu.make_async_remote_copy(
            src_ref=src, dst_ref=dst, send_sem=ss.at[slot], recv_sem=rs.at[slot],
            device_id=device, device_id_type=MESH,
        )

    def loop(low, high, body):
        def step(i, carry):
            body(i)
            return carry
        lax.fori_loop(low, high, step, 0)

    def far_first(i):
        j = (i + 1) // 2
        return 8 + j * (2 * lax.rem(i, 2) - 1)

    barrier = pltpu.get_barrier_semaphore()

    def greet(device):
        pl.semaphore_signal(barrier, inc=1, device_id=device, device_id_type=MESH)

    loop(1, 4, lambda k: greet((r, lax.rem(q + k, 4))))
    loop(1, 16, lambda k: greet(at_z(k)))
    loop(1, 8, lambda k: greet(at_s(k)))

    wp[q] = w_own[...]
    small[q] = jnp.concatenate(
        [wb_own[...], jnp.broadcast_to(cb_own[...], (2, 128)), jnp.zeros((4, 128), F32)], axis=0
    )

    def normed_row(a):
        return jnp.concatenate(
            [normalize(pair[a, pl.ds(t, 128, stride=4), :], ln_gain[0:1], ln_shift[0:1]) for t in range(4)], axis=0
        )

    own_normed = normed_row(q)
    pl.semaphore_wait(barrier, 25)

    loop(1, 4, lambda k: remote(small.at[q], small.at[q], SMALL + k, (r, lax.rem(q + k, 4))).start())
    for layer in range(2):
        remote(w_own.at[layer], wp.at[q, layer], W_CORE + layer, other_core).start()
        remote(w_own.at[layer], wp.at[q, layer], W_X + layer, other_x).start()

    def small_wait(k):
        owner = lax.rem(q + 4 - k, 4)
        copy = remote(small.at[owner], small.at[owner], SMALL + k, other_core)
        copy.wait_recv()
        copy.wait_send()

    loop(1, 4, small_wait)
    piece = dot(small[...].reshape(32, 128), own_normed, ((1,), (1,)), highest)
    for t in range(4):
        for h in range(4):
            plane0[z, y, xh, 4 * t + h : 4 * t + h + 1, :] = piece[8 * h : 8 * h + 1, 128 * t : 128 * t + 128]

    def gather_z(plane, base):
        def start(i):
            k = far_first(i)
            remote(plane.at[z, y, xh], plane.at[z, y, xh], base + k, at_z(k)).start()
        loop(0, 15, start)

    def gather_z_wait(plane, base):
        def wait(k):
            origin = lax.rem(z + 16 - k, 16)
            copy = remote(plane.at[origin, y, xh], plane.at[origin, y, xh], base + k, at_x)
            copy.wait_recv()
            copy.wait_send()
        loop(1, 16, wait)

    def gather_slab(plane, base):
        first, second = pl.ds(0, 8), pl.ds(8, 8)

        def y_first(yy, k, device):
            ref = plane.at[:, yy, xh, first]
            return remote(ref, ref, base + 16 + k, device)

        def x_first(xx):
            ref = plane.at[:, y, xx, second]
            return remote(ref, ref, base + 21, at_x)

        def y_second(yy, k, device):
            ref = plane.at[:, yy, :, second]
            return remote(ref, ref, base + 22 + k, device)

        def x_second(xx):
            ref = plane.at[:, :, xx, first]
            return remote(ref, ref, base + 20, at_x)

        x_first(xh).start()
        loop(1, 4, lambda k: y_first(y, k, at_y(k)).start())
        x_first(1 - xh).wait_recv()
        loop(1, 4, lambda k: y_second(y, k, at_y(k)).start())
        loop(1, 4, lambda k: y_first(lax.rem(y + 4 - k, 4), k, at_x).wait_recv())
        x_second(xh).start()
        loop(1, 4, lambda k: y_second(lax.rem(y + 4 - k, 4), k, at_x).wait_recv())
        x_second(1 - xh).wait_recv()
        loop(1, 4, lambda k: y_first(y, k, at_x).wait_send())
        loop(1, 4, lambda k: y_second(y, k, at_x).wait_send())
        x_first(xh).wait_send()
        x_second(xh).wait_send()

    gather_z(plane0, GATHER[0])

    for layer in range(2):
        remote(w_own.at[layer], wp.at[q_x, layer], W_X + layer, other_x).wait_recv()
        remote(wp.at[q_x, layer], wp.at[q_x, layer], W_FWD + layer, other_core).start()

    token = lax.broadcasted_iota(jnp.int32, (8, 512), 1)
    line = lax.broadcasted_iota(jnp.int32, (8, 512), 0)
    value = jnp.where(line < 4, chain[...].astype(F32), mask[...].astype(F32))
    value = jnp.where(lax.rem(token, 4) == lax.rem(line, 4), value, 0.0)
    place = lax.broadcasted_iota(jnp.int32, (512, 128), 0) // 4 == lax.broadcasted_iota(jnp.int32, (512, 128), 1)
    marks[...] = dot(value, place.astype(F32), ((1,), (0,)), highest)

    for layer in range(2):
        remote(w_own.at[layer], wp.at[q_core, layer], W_CORE + layer, other_core).wait_recv()
        remote(w_own.at[layer], wp.at[q_far, layer], W_FWD + layer, other_core).wait_recv()
        for slot, device in ((W_CORE, other_core), (W_X, other_x)):
            remote(w_own.at[layer], wp.at[q, layer], slot + layer, device).wait_send()
        remote(wp.at[q_x, layer], wp.at[q_x, layer], W_FWD + layer, other_core).wait_send()

    def weights(layer):
        for h in range(4):
            wall[pl.ds(128 * h, 128), :] = wp[h, layer].T

    def project(a, layer):
        normed = jnp.concatenate(
            [normalize(xp[a, t], ln_gain[layer : layer + 1], ln_shift[layer : layer + 1]) for t in range(4)], axis=0
        )
        normed_q = normalize(xp[a, q], ln_gain[layer : layer + 1], ln_shift[layer : layer + 1])
        for h in range(4):
            both = dot(wall[pl.ds(128 * h + 32, 64), :], normed, ((1,), (1,)), highest)
            key_high, key_low = split(both[0:32])
            k3[a, h] = jnp.concatenate([key_high, key_high, key_low], axis=0)
            value_high, value_low = split(both[32:64])
            vb[a, h] = jnp.concatenate([value_high, value_low, jnp.ones((16, 512), BF16)], axis=0)
            query = dot(wall[pl.ds(128 * h, 32), :], normed_q, ((1,), (1,)), highest) * (1.0 / math.sqrt(32))
            query_high, query_low = split(query)
            q3[a, h] = jnp.concatenate([query_high, query_low, query_high], axis=0)
            gates[a, pl.ds(32 * h, 32), :] = jax.nn.sigmoid(
                dot(wall[pl.ds(128 * h + 96, 32), :], normed_q, ((1,), (1,)), highest)
            )

    def make_bias(layer, plane):
        chain_q = jnp.broadcast_to(marks[pl.ds(q, 1), :], (128, 128)).T
        flat = plane.reshape(2048, 128)
        for t in range(4):
            same = (chain_q == marks[t : t + 1, :]).astype(F32)
            key_bias = (marks[4 + t : 5 + t, :] - 1.0) * 1000000000.0
            for h in range(4):
                tile = flat[pl.ds(4 * t + h, 128, stride=16), :]
                if layer == 1:
                    tile = tile.T
                bias[h, :, 128 * t : 128 * t + 128] = tile + small[h, 2 + layer : 3 + layer, :] * same + key_bias

    def attend(a, layer):
        heads = []
        for h in range(4):
            score = dot(q3[a, h], k3[a, h], ((0,), (0,))) + bias[h]
            weight = jnp.exp(score - jnp.max(score, axis=-1, keepdims=True))
            weight_high, weight_low = split(weight)
            total = dot(vb[a, h], weight_high, ((1,), (1,))) + dot(vb[a, h], weight_low, ((1,), (1,)))
            heads.append((total[0:32] + total[32:64]) / total[64:65] * gates[a, pl.ds(32 * h, 32), :])
        joined = jnp.concatenate(heads, axis=0)
        return xp[a, q] + dot(joined, w_out[layer], ((0,), (0,)), highest)

    def permute_row(a):
        for t in range(4):
            xp[a, t] = pair[a, pl.ds(t, 128, stride=4), :]

    weights(0)

    def first_project(a):
        permute_row(a)
        project(a, 0)

    loop(0, 4, first_project)
    gather_z_wait(plane0, GATHER[0])
    gather_slab(plane0, GATHER[0])
    make_bias(0, plane0)

    def first_attend(a):
        row = attend(a, 0)
        after[a] = row
        normed = normalize(row, ln_gain[1:2], ln_shift[1:2])
        mine = dot(small[...].reshape(32, 128), normed, ((1,), (1,)), highest)
        for h in range(4):
            plane1[z, y, xh, pl.ds(4 * a + h, 1), :] = mine[8 * h + 1 : 8 * h + 2, :]

    loop(0, 4, first_attend)

    def pair_z(i):
        k = far_first(i)
        there = lax.rem(z + k, 16)
        remote(after.at[:, pl.ds(pl.multiple_of(there * 8, 8), 8)], mid.at[:, z], PAIR_Z + k, at_z(k)).start()

    loop(0, 15, pair_z)
    gather_z(plane1, GATHER[1])
    mid[:, z] = after[:, pl.ds(pl.multiple_of(z * 8, 8), 8), :]
    weights(1)

    def pair_z_wait(k):
        origin = lax.rem(z + 16 - k, 16)
        copy = remote(after.at[:, pl.ds(0, 8)], mid.at[:, origin], PAIR_Z + k, at_x)
        copy.wait_recv()
        copy.wait_send()

    loop(1, 16, pair_z_wait)
    for a in range(4):
        flat_mid = mid.at[a].reshape(128, 128)
        for there in range(8):
            mid2[there, 16 * a : 16 * a + 16, :] = flat_mid[pl.ds(there, 16, stride=8), :]

    def pair_s(k):
        there = lax.rem(s + k, 8)
        remote(mid2.at[there], cols.at[q, s], PAIR_S + k, at_s(k)).start()

    loop(1, 8, pair_s)
    cols[q, s] = mid2[s]

    def share(origin):
        block = cols.at[q, origin]
        remote(block, block, COL_CORE + origin, other_core).start()
        remote(block, block, COL_X + origin, other_x).start()

    share(s)

    def pair_s_wait(k):
        origin = lax.rem(s + 8 - k, 8)
        copy = remote(mid2.at[0], cols.at[q, origin], PAIR_S + k, at_x)
        copy.wait_recv()
        copy.wait_send()
        share(origin)

    loop(1, 8, pair_s_wait)

    def pass_on(origin):
        block = cols.at[q_x, origin]
        remote(block, block, COL_X + origin, other_x).wait_recv()
        remote(block, block, COL_FWD + origin, other_core).start()

    loop(0, 8, pass_on)

    def permute_col(c):
        flat = cols.at[c].reshape(512, 128)
        for a in range(4):
            xp[c, a] = jnp.concatenate(
                [flat[pl.ds(16 * a + zz, 8, stride=64), :] for zz in range(16)], axis=0
            )

    def second_project(c):
        permute_col(c)
        project(c, 1)

    second_project(q)
    second_project(q_x)

    def share_wait(origin):
        block = cols.at[q, origin]
        remote(block, cols.at[q_core, origin], COL_CORE + origin, other_core).wait_recv()
        remote(block, block, COL_CORE + origin, other_core).wait_send()
        remote(block, block, COL_X + origin, other_x).wait_send()

    loop(0, 8, share_wait)
    second_project(q_core)

    def forward_wait(origin):
        block = cols.at[q_far, origin]
        remote(block, block, COL_FWD + origin, other_core).wait_recv()
        block = cols.at[q_x, origin]
        remote(block, block, COL_FWD + origin, other_core).wait_send()

    loop(0, 8, forward_wait)
    second_project(q_far)
    gather_z_wait(plane1, GATHER[1])
    gather_slab(plane1, GATHER[1])
    make_bias(1, plane1)

    def second_attend(c):
        out[c, q] = attend(c, 1)
        block = out.at[c, q]
        remote(block, block, OUT_X + c, other_x).start()
        remote(block, block, OUT_CORE + c, other_core).start()

    loop(0, 4, second_attend)

    def out_pass_on(c):
        block = out.at[c, q_x]
        remote(block, block, OUT_X + c, other_x).wait_recv()
        remote(block, block, OUT_FWD + c, other_core).start()

    loop(0, 4, out_pass_on)

    def out_wait(c):
        remote(out.at[c, q_core], out.at[c, q_core], OUT_CORE + c, other_core).wait_recv()
        remote(out.at[c, q_far], out.at[c, q_far], OUT_FWD + c, other_core).wait_recv()
        remote(out.at[c, q], out.at[c, q], OUT_X + c, other_x).wait_send()
        remote(out.at[c, q], out.at[c, q], OUT_CORE + c, other_core).wait_send()
        remote(out.at[c, q_x], out.at[c, q_x], OUT_FWD + c, other_core).wait_send()

    loop(0, 4, out_wait)


def shards(pair_rep, residue_mask, chain_ids, ln_gain, ln_shift, w_proj, w_bias, chain_bias, w_out):
    vmem = pl.BlockSpec(memory_space=pltpu.VMEM)
    result = pl.pallas_call(
        kernel,
        out_shape=jax.ShapeDtypeStruct((4, 4, 128, 128), F32),
        in_specs=[vmem] * 9,
        out_specs=vmem,
        scratch_shapes=[
            pltpu.VMEM((4, 4, 128, 128), F32),
            pltpu.VMEM((4, 2, 128, 128), F32),
            pltpu.VMEM((4, 8, 128), F32),
            pltpu.VMEM((16, 4, 2, 16, 128), F32),
            pltpu.VMEM((16, 4, 2, 16, 128), F32),
            pltpu.VMEM((4, 128, 128), F32),
            pltpu.VMEM((4, 16, 8, 128), F32),
            pltpu.VMEM((8, 64, 128), F32),
            pltpu.VMEM((4, 8, 64, 128), F32),
            pltpu.VMEM((4, 4, 96, 512), BF16),
            pltpu.VMEM((4, 4, 96, 128), BF16),
            pltpu.VMEM((4, 4, 80, 512), BF16),
            pltpu.VMEM((4, 128, 128), F32),
            pltpu.VMEM((4, 128, 512), F32),
            pltpu.VMEM((512, 128), F32),
            pltpu.VMEM((8, 128), F32),
            pltpu.SemaphoreType.DMA((SLOTS,)),
            pltpu.SemaphoreType.DMA((SLOTS,)),
        ],
        compiler_params=pltpu.CompilerParams(
            collective_id=0, has_side_effects=True, vmem_limit_bytes=40 * 1024 * 1024
        ),
    )(
        pair_rep,
        residue_mask.reshape(1, 512),
        chain_ids.reshape(1, 512),
        ln_gain,
        ln_shift,
        w_proj.reshape(2, 128, 128),
        w_bias.reshape(2, 128),
        chain_bias,
        w_out,
    )
    return jnp.transpose(result, (2, 1, 0, 3)).reshape(512, 4, 128)


def solution(mesh):
    in_specs = (
        P("row", None, None),
        P(),
        P(),
        P(),
        P(),
        P(None, None, "head", None),
        P(None, None, "head"),
        P(None, "head"),
        P(),
    )
    return jax.shard_map(shards, mesh=mesh, in_specs=in_specs, out_specs=P(None, "row", None), check_vma=False)
```

time: 586 us -> 122 us (0.21)
  waiting for transfers between devices: 432 us -> 0 us
  Pallas kernels: 0 us -> 114 us
  blocking collectives: 68 us -> 0 us
  matrix products: 45.2 us -> 0 us
  other arithmetic: 13.5 us -> 0 us
  between operations: 13.4 us -> 0.05 us
    all_gather x4 -> x0, waiting for transfers between devices: 432 us -> none  [the longest x1 187 us: shards(): plane_piece = lax.all_gather(plane_rows, 'row', axis=1, tiled=True)]
    pallas_call x0 -> x1, Pallas kernels: none -> 114 us  [shards(): pl.pallas_call(kernel, out_shape=jax.ShapeDtypeStruct((4, 4, 128, 128), F...]
    all_to_all x1 -> x0, blocking collectives: 68 us -> none  [shards(): lax.all_to_all(after_start, 'row', split_axis=1, concat_axis=0, tiled=True)]
    dot_general x22 -> x0, matrix products: 45.2 us -> none  [the longest x4 9.35 us: one_row(): jnp.einsum('hjk,khd->jhd', weights, value_row, precision=highest) * gate_row]
  transfers between devices with their start and end apart: 4 -> 0, of which waited for: 4 -> 0; matrix products, arithmetic and copies ran while one was open for 1% -> 0% of each run, Pallas kernels for 0% -> 0%
where the time goes in v1:
time: 122 us; the launch traced here: 121 us
  Pallas kernels  114 us (93%)
  local copies, waits for them, and re-layouts  6.69 us (5%)
    pallas_call x1, Pallas kernels, shards(): pl.pallas_call(kernel, out_shape=jax.ShapeDtypeStruct((4, 4, 128, 128), F...  114 us
    unnamed x19, local copies, waits for them, and re-layouts  4.37 us

profile of v1, /device:TPU:1, one launch (start us, length us, event | category | flops | bytes accessed | tf_op | source)
XLA Modules:
  0.0 121.2 jit_solution(2449507555217347165)
XLA Ops:
  0.0 0.0 copy-start.6
  0.0 0.0 copy-start.7
  0.0 0.0 copy-start.8
  0.0 0.0 copy-start.4
  0.0 0.0 copy-start.3
  0.0 0.7 copy-done.8
  0.7 0.0 copy-start.5
  0.7 0.1 copy.11.cb_own
  0.8 0.0 copy-done.6
  0.8 0.0 copy-done.7
  0.8 0.0 copy-done.4
  0.8 0.0 copy-done.3
  0.8 0.6 copy-done.5
  1.4 0.0 copy-start
  1.4 1.2 %copy-done = f32[4,512,128]{2,1,0:T(8,128)S(1)} copy-done((f32[4,512,128]{2,1,0:T(8,128)S(1)}, f32[4,512,128]{2,1,0:T(8,128)}, u32[]{:S(2)}) %copy-start) | copy-done | bytes 1048600
  2.6 0.0 copy-start.1
  2.6 0.9 copy-done.1
  3.5 0.0 copy-start.2
  3.5 0.9 copy-done.2
  4.4 114.5 %shard_map.91 = f32[4,4,128,128]{3,2,1,0:T(8,128)S(1)} custom-call(f32[4,512,128]{2,1,0:T(8,128)S(1)} %copy-done, s32[1,512]{1,0:T(1,128)S(1)} %bitcast.8, s32[1,512]{1,0:T(1,128)S(1)} %bitcast.9, f32[2,128]{1,0:T(2,128)S(1)} %copy-done.5, f32[2,128]{1,0:T(2,128)S(1)} %copy-done.6, f32[2,128,128]{2,1,0:T(8,128)S(1)} %bitcast.7, f32[2,128]{1,0:T(2,128)S(1)} %bitcast.10, ...), custom_call_target="tpu_custom_call" | custom-call | tf_op jit(solution)/shard_map/pallas_call | solution.py:367
  118.9 0.7 copy.12
  119.6 1.6 %copy.13 = f32[512,4,128]{2,1,0:T(4,128)} copy(f32[512,4,128]{2,0,1:T(8,128)S(1)} %bitcast.11) | data formatting | bytes 2097152 | tf_op jit(solution)/shard_map/reshape | solution.py:406
Async XLA Ops:
  0.0 0.8 copy-start.6
  0.0 0.8 copy-start.7
  0.0 0.7 copy-start.8
  0.0 0.8 copy-start.4
  0.0 0.8 copy-start.3
  0.7 0.7 copy-start.5
  1.4 1.2 %copy-start = (f32[4,512,128]{2,1,0:T(8,128)S(1)}, f32[4,512,128]{2,1,0:T(8,128)}, u32[]{:S(2)}) copy-start(f32[4,512,128]{2,1,0:T(8,128)} %pair.1) | copy-start | bytes 3145732
  2.6 0.9 copy-start.1
  3.5 0.9 copy-start.2

commit v2 on v0

v2 whole, which is shorter than its diff:
```python
import functools
import math

import jax
import jax.numpy as jnp
from jax import lax
from jax.experimental import pallas as pl
from jax.experimental.pallas import tpu as pltpu
from jax.sharding import PartitionSpec as P

highest = lax.Precision.HIGHEST
MESH = pl.DeviceIdType.MESH
F32, BF16 = jnp.float32, jnp.bfloat16

class Slots:
    def __init__(self):
        self.count = 0

    def take(self, number):
        self.count += number
        return self.count - number


arrive = Slots()
PLANE_Z = (arrive.take(4), arrive.take(8))
Y_FIRST, X_FIRST, Y_SECOND, X_SECOND = ([arrive.take(4) for _ in range(2)] for _ in range(4))
PAIR_Z, PAIR_S = arrive.take(4), arrive.take(4)
COL_CORE, COL_X, COL_FWD = arrive.take(4), arrive.take(4), arrive.take(4)
OUT_CORE, OUT_X, OUT_FWD = arrive.take(4), arrive.take(4), arrive.take(4)
SMALL, W_CORE, W_X, W_FWD = arrive.take(1), arrive.take(1), arrive.take(1), arrive.take(1)
LOCAL = OUT_CORE
leave = Slots()
LEFT_Z = (leave.take(1), leave.take(1))
LEFT_YX = (leave.take(1), leave.take(1))
LEFT_PAIR_Z, LEFT_PAIR_S, LEFT_COL, LEFT_OUT, LEFT_W, LEFT_SMALL = (leave.take(1) for _ in range(6))


def dot(a, b, dims, precision=None):
    return lax.dot_general(a, b, (dims, ((), ())), precision=precision, preferred_element_type=F32)


def split(x):
    high = x.astype(BF16)
    return high, (x - high.astype(F32)).astype(BF16)


def normalize(x, gain, shift):
    centred = x - jnp.mean(x, axis=-1, keepdims=True)
    spread = jnp.mean(centred * centred, axis=-1, keepdims=True)
    return centred * lax.rsqrt(spread + 1e-05) * gain + shift


def kernel(
    pair_in, mask_in, chain_in, gain_in, shift_in, w_own, wb_in, cb_in, w_out_in, out,
    pair, mask, chain, ln_gain, ln_shift, wb_own, cb_own, w_out,
    xp, wp, small, plane0, plane1, after, mid, mid2, cols, k3, q3, vb, gates, bias, wkv, wqg, marks, outs, ss, rs,
):
    r, q = lax.axis_index("row"), lax.axis_index("head")
    z, s = r // 8, lax.rem(r, 8)
    y, xh = s // 2, lax.rem(s, 2)
    core, xlo = lax.rem(q, 2), q // 2
    other_core = (r, xlo * 2 + 1 - core)
    other_x = (r, (1 - xlo) * 2 + core)
    q_core, q_x = other_core[1], other_x[1]
    q_far = (1 - xlo) * 2 + 1 - core

    def at_z(k):
        return (lax.rem(z + k, 16) * 8 + s, q)

    def at_y(k):
        return (z * 8 + lax.rem(y + k, 4) * 2 + xh, q)

    def at_s(k):
        return (z * 8 + lax.rem(s + k, 8), q)

    at_x = (z * 8 + y * 2 + 1 - xh, q)

    def send(src, dst, left, slot, device):
        pltpu.make_async_remote_copy(
            src_ref=src, dst_ref=dst, send_sem=ss.at[left], recv_sem=rs.at[slot],
            device_id=device, device_id_type=MESH,
        ).start()

    def arrived(ref, slot):
        pltpu.make_async_remote_copy(
            src_ref=ref, dst_ref=ref, send_sem=ss.at[0], recv_sem=rs.at[slot],
            device_id=at_x, device_id_type=MESH,
        ).wait_recv()

    def left(ref, slot):
        pltpu.make_async_remote_copy(
            src_ref=ref, dst_ref=ref, send_sem=ss.at[slot], recv_sem=rs.at[0],
            device_id=at_x, device_id_type=MESH,
        ).wait_send()

    def loop(low, high, body):
        def step(i, carry):
            body(i)
            return carry
        lax.fori_loop(low, high, step, 0)

    def far_first(i):
        j = (i + 1) // 2
        return 8 + j * (2 * lax.rem(i, 2) - 1)

    local = [
        pltpu.make_async_copy(pair_in.at[q], pair.at[q], rs.at[LOCAL]),
        pltpu.make_async_copy(gain_in, ln_gain, rs.at[LOCAL + 1]),
        pltpu.make_async_copy(shift_in, ln_shift, rs.at[LOCAL + 2]),
        pltpu.make_async_copy(wb_in, wb_own, rs.at[LOCAL + 3]),
        pltpu.make_async_copy(cb_in, cb_own, rs.at[LOCAL + 4]),
        pltpu.make_async_copy(w_own, wp.at[q], rs.at[LOCAL + 5]),
        pltpu.make_async_copy(mask_in, mask, rs.at[LOCAL + 6]),
        pltpu.make_async_copy(chain_in, chain, rs.at[LOCAL + 7]),
        pltpu.make_async_copy(w_out_in, w_out, rs.at[LOCAL + 8]),
    ] + [
        pltpu.make_async_copy(
            pair_in.at[lax.rem(q + k, 4)], pair.at[lax.rem(q + k, 4)], rs.at[LOCAL + 8 + k]
        )
        for k in range(1, 4)
    ]
    for copy in local[:6]:
        copy.start()

    barrier = pltpu.get_barrier_semaphore()

    def greet(device):
        pl.semaphore_signal(barrier, inc=1, device_id=device, device_id_type=MESH)

    loop(1, 4, lambda k: greet((r, lax.rem(q + k, 4))))
    loop(0, 15, lambda i: greet(at_z(far_first(i))))
    loop(1, 8, lambda k: greet(at_s(k)))
    for copy in local[6:]:
        copy.start()
    for copy in local[:6]:
        copy.wait()
    small[q] = jnp.concatenate(
        [
            wb_own[...],
            jnp.broadcast_to(cb_own[0:1, 0:1], (1, 128)),
            jnp.broadcast_to(cb_own[0:1, 1:2], (1, 128)),
            jnp.zeros((4, 128), F32),
        ],
        axis=0,
    )
    pl.semaphore_wait(barrier, 25)

    loop(1, 4, lambda k: send(small.at[q], small.at[q], LEFT_SMALL, SMALL, (r, lax.rem(q + k, 4))))
    send(wp.at[q], wp.at[q], LEFT_W, W_X, other_x)
    send(wp.at[q], wp.at[q], LEFT_W, W_CORE, other_core)

    own_normed = jnp.concatenate(
        [normalize(pair[q, pl.ds(t, 128, stride=4), :], ln_gain[0:1], ln_shift[0:1]) for t in range(4)], axis=0
    )

    arrived(small.at[0:3], SMALL)
    piece = dot(small[...].reshape(32, 128), own_normed, ((1,), (1,)), highest)
    for t in range(4):
        for h in range(4):
            plane0[8, y, xh, 4 * t + h : 4 * t + h + 1, :] = piece[8 * h : 8 * h + 1, 128 * t : 128 * t + 128]

    first, second = pl.ds(0, 8), pl.ds(8, 8)
    planes = (plane0, plane1)

    def quarter(i):
        j = (i + 1) // 2
        return 2 + j * (1 - 2 * lax.rem(i, 2))

    def gather_z(layer, half, lines):
        def start(i):
            place = quarter(i // 4) * 4 + lax.rem(i, 4)
            send(
                planes[layer].at[8, y, xh, lines], planes[layer].at[place, y, xh, lines],
                LEFT_Z[layer], PLANE_Z[layer] + 4 * half + i // 4, at_z(lax.rem(24 - place, 16)),
            )
        loop(1, 16, start)

    def gather_z_wait(layer, half, lines, i):
        slot = PLANE_Z[layer] + 4 * half + i

        @pl.when(i == 0)
        def _():
            arrived(planes[layer].at[9:12, y, xh, lines], slot)

        @pl.when(i > 0)
        def _():
            arrived(planes[layer].at[pl.ds(quarter(i) * 4, 4), y, xh, lines], slot)

    def around(i):
        return pl.ds(quarter(i) * 4, 4)

    def start_yx(layer, i):
        ref = planes[layer].at[around(i), y, xh, first]
        loop(1, 4, lambda k: send(ref, ref, LEFT_YX[layer], Y_FIRST[layer] + i, at_y(k)))

    def start_xy(layer, i):
        ref = planes[layer].at[around(i), y, xh, second]
        send(ref, ref, LEFT_YX[layer], X_FIRST[layer] + i, at_x)

    def next_yx(layer, i):
        arrived(planes[layer].at[around(i), 0:3, xh, first], Y_FIRST[layer] + i)
        ref = planes[layer].at[around(i), :, xh, first]
        send(ref, ref, LEFT_YX[layer], X_SECOND[layer] + i, at_x)

    def next_xy(layer, i):
        arrived(planes[layer].at[around(i), y, xh, second], X_FIRST[layer] + i)
        ref = planes[layer].at[around(i), y, :, second]
        loop(1, 4, lambda k: send(ref, ref, LEFT_YX[layer], Y_SECOND[layer] + i, at_y(k)))

    def finish(layer):
        def wait(i):
            arrived(planes[layer].at[around(i), 0:3, :, second], Y_SECOND[layer] + i)
            arrived(planes[layer].at[around(i), :, xh, first], X_SECOND[layer] + i)
        loop(0, 4, wait)

    both = pl.ds(0, 16)
    gather_z(0, 0, both)

    arrived(wp.at[q_x], W_X)
    send(wp.at[q_x], wp.at[q_x], LEFT_W, W_FWD, other_core)

    for copy in local[6:]:
        copy.wait()
    token = lax.broadcasted_iota(jnp.int32, (8, 512), 1)
    line = lax.broadcasted_iota(jnp.int32, (8, 512), 0)
    value = jnp.where(line < 4, chain[...].astype(F32), mask[...].astype(F32))
    value = jnp.where(lax.rem(token, 4) == lax.rem(line, 4), value, 0.0)
    place = lax.broadcasted_iota(jnp.int32, (512, 128), 0) // 4 == lax.broadcasted_iota(jnp.int32, (512, 128), 1)
    marks[...] = dot(value, place.astype(F32), ((1,), (0,)), highest)

    arrived(wp.at[q_core], W_CORE)
    arrived(wp.at[q_far], W_FWD)

    def weights(layer):
        for h in range(4):
            turned = wp[h, layer].T
            for ref, rows in ((wkv, turned[32:96]), (wqg, jnp.concatenate([turned[0:32], turned[96:128]], axis=0))):
                high, low = split(rows)
                ref[pl.ds(64 * h, 64), :] = jnp.concatenate([high, low], axis=1)

    def multiply(weight, features):
        high, low = split(features)
        doubled = jnp.concatenate([high, high], axis=1)
        return dot(weight[...], doubled, ((1,), (1,))) + dot(weight[:, 0:128], low, ((1,), (1,)))

    def project(a, layer):
        gain, shift = ln_gain[layer : layer + 1], ln_shift[layer : layer + 1]
        keyed = multiply(wkv, jnp.concatenate([normalize(xp[a, t], gain, shift) for t in range(4)], axis=0))
        asked = multiply(wqg, normalize(xp[a, q], gain, shift))
        for h in range(4):
            key_high, key_low = split(keyed[64 * h : 64 * h + 32])
            k3[a, h] = jnp.concatenate([key_high, key_high, key_low], axis=0)
            value_high, value_low = split(keyed[64 * h + 32 : 64 * h + 64])
            vb[a, h] = jnp.concatenate([value_high, value_low, jnp.ones((16, 512), BF16)], axis=0)
            query_high, query_low = split(asked[64 * h : 64 * h + 32] * (1.0 / math.sqrt(32)))
            q3[a, h] = jnp.concatenate([query_high, query_low, query_high], axis=0)
            gates[a, pl.ds(32 * h, 32), :] = jax.nn.sigmoid(asked[64 * h + 32 : 64 * h + 64])

    def make_bias(layer):
        chain_q = jnp.broadcast_to(marks[pl.ds(q, 1), :], (128, 128)).T
        flat = planes[layer].reshape(16, 128, 128)
        for t in range(4):
            same = (chain_q == marks[t : t + 1, :]).astype(F32)
            key_bias = (marks[4 + t : 5 + t, :] - 1.0) * 1000000000.0
            for h in range(4):
                tile = jnp.concatenate(
                    [flat[lax.rem(zz + 24 - z, 16), pl.ds(4 * t + h, 8, stride=16), :] for zz in range(16)], axis=0
                )
                if layer == 1:
                    tile = tile.T
                bias[h, :, 128 * t : 128 * t + 128] = tile + small[h, 2 + layer : 3 + layer, :] * same + key_bias

    def attend(a, layer):
        heads = []
        for h in range(4):
            score = dot(q3[a, h], k3[a, h], ((0,), (0,))) + bias[h]
            weight = jnp.exp(score - jnp.max(score, axis=-1, keepdims=True))
            weight_high, weight_low = split(weight)
            total = dot(vb[a, h], weight_high, ((1,), (1,))) + dot(vb[a, h], weight_low, ((1,), (1,)))
            heads.append((total[0:32] + total[32:64]) / total[64:65] * gates[a, pl.ds(32 * h, 32), :])
        joined = jnp.concatenate(heads, axis=0)
        return xp[a, q] + dot(joined, w_out[layer], ((0,), (0,)), highest)

    weights(0)

    def first_project(a):
        gather_z_wait(0, 0, both, a)
        start_yx(0, a)
        start_xy(0, a)
        for t in range(4):
            xp[a, t] = pair[a, pl.ds(t, 128, stride=4), :]
        project(a, 0)

        @pl.when(a > 0)
        def _():
            next_xy(0, a - 1)
            next_yx(0, a - 1)

    loop(0, 4, first_project)
    next_xy(0, 3)
    next_yx(0, 3)
    finish(0)
    make_bias(0)

    def first_attend(a):
        row = attend(a, 0)
        after[a] = row

        def leave_z(i):
            k = far_first(i)
            rows = pl.ds(pl.multiple_of(lax.rem(z + k, 16) * 8, 8), 8)
            send(after.at[a, rows], mid.at[a, z], LEFT_PAIR_Z, PAIR_Z + a, at_z(k))

        loop(0, 15, leave_z)
        mid[a, z] = after[a, pl.ds(pl.multiple_of(z * 8, 8), 8), :]
        normed = normalize(row, ln_gain[1:2], ln_shift[1:2])
        mine = dot(small[...].reshape(32, 128), normed, ((1,), (1,)), highest)
        for h in range(4):
            plane1[8, y, xh, pl.ds(4 * a + h, 1), :] = mine[8 * h + 1 : 8 * h + 2, :]

    loop(0, 2, first_attend)
    gather_z(1, 0, first)
    loop(2, 4, first_attend)
    gather_z(1, 1, second)
    weights(1)

    def over_slab(a):
        arrived(mid.at[a, 0:15], PAIR_Z + a)
        flat = mid.at[a].reshape(128, 128)
        for there in range(8):
            mid2[a, there] = flat[pl.ds(there, 16, stride=8), :]

        def leave_s(k):
            send(mid2.at[a, lax.rem(s + k, 8)], cols.at[q, s, a], LEFT_PAIR_S, PAIR_S + a, at_s(k))

        loop(1, 8, leave_s)
        cols[q, s, a] = mid2[a, s]

    def share(a):
        arrived(cols.at[q, 0:7, a], PAIR_S + a)
        block = cols.at[q, :, a]
        send(block, block, LEFT_COL, COL_X + a, other_x)
        send(block, block, LEFT_COL, COL_CORE + a, other_core)

    def pass_on(a):
        block = cols.at[q_x, :, a]
        arrived(block, COL_X + a)
        send(block, block, LEFT_COL, COL_FWD + a, other_core)

    def half_first(i):
        gather_z_wait(1, 0, first, i)
        start_yx(1, i)

    def half_second(i):
        gather_z_wait(1, 1, second, i)
        start_xy(1, i)

    def second_project(c):
        flat = cols.at[c].reshape(512, 128)
        for a in range(4):
            xp[c, a] = jnp.concatenate([flat[pl.ds(16 * a + zz, 8, stride=64), :] for zz in range(16)], axis=0)
        project(c, 1)

    over_slab(0)
    over_slab(1)
    share(0)
    loop(0, 4, half_first)
    over_slab(2)
    share(1)
    pass_on(0)
    loop(0, 4, lambda i: next_yx(1, i))
    over_slab(3)
    share(2)
    pass_on(1)
    loop(0, 4, half_second)
    share(3)
    pass_on(2)
    loop(0, 4, lambda i: next_xy(1, i))

    def own_column(i):
        @pl.when(i == 1)
        def _():
            pass_on(3)
            loop(0, 4, lambda a: arrived(cols.at[q_core, :, a], COL_CORE + a))

        @pl.when(i == 3)
        def _():
            loop(0, 4, lambda a: arrived(cols.at[q_far, :, a], COL_FWD + a))

        second_project(jnp.where(i == 0, q, jnp.where(i == 1, q_x, jnp.where(i == 2, q_core, q_far))))

    loop(0, 4, own_column)

    finish(1)
    make_bias(1)

    def out_pass_on(c):
        block = outs.at[c, q_x]
        arrived(block, OUT_X + c)
        send(block, block, LEFT_OUT, OUT_FWD + c, other_core)
        out[pl.ds(4 * q_x + c, 128, stride=16), :] = outs[c, q_x]
        arrived(outs.at[c, q_core], OUT_CORE + c)
        out[pl.ds(4 * q_core + c, 128, stride=16), :] = outs[c, q_core]

    def second_attend(c):
        result = attend(c, 1)
        outs[c, q] = result
        block = outs.at[c, q]
        send(block, block, LEFT_OUT, OUT_X + c, other_x)
        send(block, block, LEFT_OUT, OUT_CORE + c, other_core)
        out[pl.ds(4 * q + c, 128, stride=16), :] = result

        @pl.when(c > 1)
        def _():
            out_pass_on(c - 2)

    loop(0, 4, second_attend)
    loop(2, 4, out_pass_on)

    def out_end(c):
        arrived(outs.at[c, q_far], OUT_FWD + c)
        out[pl.ds(4 * q_far + c, 128, stride=16), :] = outs[c, q_far]

    loop(0, 4, out_end)

    left(small.at[0:3], LEFT_SMALL)
    left(wp.at[0:3], LEFT_W)
    for layer in range(2):
        left(planes[layer].at[0:15, 0, 0], LEFT_Z[layer])
        left(planes[layer].at[0:14], LEFT_YX[layer])
    left(mid.at[:, 0:15], LEFT_PAIR_Z)
    left(mid2.at[:, 0:7], LEFT_PAIR_S)
    left(cols.at[0:3], LEFT_COL)
    left(outs.at[0:3], LEFT_OUT)


def shards(pair_rep, residue_mask, chain_ids, ln_gain, ln_shift, w_proj, w_bias, chain_bias, w_out):
    vmem = pl.BlockSpec(memory_space=pltpu.VMEM)
    hbm = pl.BlockSpec(memory_space=pltpu.HBM)
    result = pl.pallas_call(
        kernel,
        out_shape=jax.ShapeDtypeStruct((2048, 128), F32),
        in_specs=[hbm] * 9,
        out_specs=vmem,
        scratch_shapes=[
            pltpu.VMEM((4, 512, 128), F32),
            pltpu.VMEM((1, 512), jnp.int32),
            pltpu.VMEM((1, 512), jnp.int32),
            pltpu.VMEM((2, 128), F32),
            pltpu.VMEM((2, 128), F32),
            pltpu.VMEM((2, 128), F32),
            pltpu.VMEM((1, 2), F32),
            pltpu.VMEM((2, 128, 128), F32),
            pltpu.VMEM((4, 4, 128, 128), F32),
            pltpu.VMEM((4, 2, 128, 128), F32),
            pltpu.VMEM((4, 8, 128), F32),
            pltpu.VMEM((16, 4, 2, 16, 128), F32),
            pltpu.VMEM((16, 4, 2, 16, 128), F32),
            pltpu.VMEM((4, 128, 128), F32),
            pltpu.VMEM((4, 16, 8, 128), F32),
            pltpu.VMEM((4, 8, 16, 128), F32),
            pltpu.VMEM((4, 8, 4, 16, 128), F32),
            pltpu.VMEM((4, 4, 96, 512), BF16),
            pltpu.VMEM((4, 4, 96, 128), BF16),
            pltpu.VMEM((4, 4, 80, 512), BF16),
            pltpu.VMEM((4, 128, 128), F32),
            pltpu.VMEM((4, 128, 512), F32),
            pltpu.VMEM((256, 256), BF16),
            pltpu.VMEM((256, 256), BF16),
            pltpu.VMEM((8, 128), F32),
            pltpu.VMEM((4, 4, 128, 128), F32),
            pltpu.SemaphoreType.DMA((leave.count,)),
            pltpu.SemaphoreType.DMA((arrive.count,)),
        ],
        compiler_params=pltpu.CompilerParams(
            collective_id=0, has_side_effects=True, vmem_limit_bytes=40 * 1024 * 1024
        ),
    )(
        *(
            pltpu.with_memory_space_constraint(operand, pltpu.HBM)
            for operand in (
                pair_rep,
                residue_mask.reshape(1, 512),
                chain_ids.reshape(1, 512),
                ln_gain,
                ln_shift,
                w_proj.reshape(2, 128, 128),
                w_bias.reshape(2, 128),
                chain_bias.reshape(1, 2),
                w_out,
            )
        )
    )
    return result.reshape(512, 4, 128)


def solution(mesh):
    in_specs = (
        P("row", None, None),
        P(),
        P(),
        P(),
        P(),
        P(None, None, "head", None),
        P(None, None, "head"),
        P(None, "head"),
        P(),
    )
    return jax.shard_map(shards, mesh=mesh, in_specs=in_specs, out_specs=P(None, "row", None), check_vma=False)
```

time: 586 us -> 89.4 us (0.15)
  waiting for transfers between devices: 432 us -> 0 us
  Pallas kernels: 0 us -> 88.3 us
  blocking collectives: 68 us -> 0 us
  matrix products: 45.2 us -> 0 us
  other arithmetic: 13.5 us -> 0 us
  between operations: 13.4 us -> 0.01 us
  local copies, waits for them, and re-layouts: 12.4 us -> 0.97 us
    all_gather x4 -> x0, waiting for transfers between devices: 432 us -> none  [the longest x1 187 us: shards(): plane_piece = lax.all_gather(plane_rows, 'row', axis=1, tiled=True)]
    pallas_call x0 -> x1, Pallas kernels: none -> 88.3 us  [shards(): pl.pallas_call(kernel, out_shape=jax.ShapeDtypeStruct((2048, 128), F32),...]
    all_to_all x1 -> x0, blocking collectives: 68 us -> none  [shards(): lax.all_to_all(after_start, 'row', split_axis=1, concat_axis=0, tiled=True)]
    dot_general x22 -> x0, matrix products: 45.2 us -> none  [the longest x4 9.35 us: one_row(): jnp.einsum('hjk,khd->jhd', weights, value_row, precision=highest) * gate_row]
  transfers between devices with their start and end apart: 4 -> 0, of which waited for: 4 -> 0; matrix products, arithmetic and copies ran while one was open for 1% -> 0% of each run, Pallas kernels for 0% -> 0%
where the time goes in v2:
time: 89.4 us; the launch traced here: 89.3 us
  Pallas kernels  88.3 us (99%)
  local copies, waits for them, and re-layouts  0.97 us (1%)
    pallas_call x1, Pallas kernels, shards(): pl.pallas_call(kernel, out_shape=jax.ShapeDtypeStruct((2048, 128), F32),...  88.3 us

profile of v2, /device:TPU:1, one launch (start us, length us, event | category | flops | bytes accessed | tf_op | source)
XLA Modules:
  0.0 89.3 jit_solution(17282259309476444087)
XLA Ops:
  0.0 88.3 %shard_map.91 = f32[2048,128]{1,0:T(8,128)S(1)} custom-call(f32[4,512,128]{2,1,0:T(8,128)} %pair_in.1, s32[1,512]{1,0:T(1,128)} %bitcast.8, s32[1,512]{1,0:T(1,128)} %bitcast.9, f32[2,128]{1,0:T(2,128)} %gain_in.1, f32[2,128]{1,0:T(2,128)} %shift_in.1, f32[2,128,128]{2,1,0:T(8,128)} %bitcast.7, f32[2,128]{1,0:T(2,128)} %bitcast.10, f32[1,2]{1,0:T(1,128)} %bitcast.11, ...), custom_call_target="tpu_custom_call" | custom-call | tf_op jit(solution)/shard_map/pallas_call | solution.py:440
  88.3 1.0 %copy.11 = f32[512,4,128]{2,1,0:T(4,128)} copy(f32[512,4,128]{2,1,0:T(4,128)S(1)} %bitcast.6) | data formatting | bytes 2097152

commit v3 on v2

--- a/solution.py
+++ b/solution.py
@@ -53,27 +53,33 @@
 def kernel(
     pair_in, mask_in, chain_in, gain_in, shift_in, w_own, wb_in, cb_in, w_out_in, out,
     pair, mask, chain, ln_gain, ln_shift, wb_own, cb_own, w_out,
-    xp, wp, small, plane0, plane1, after, mid, mid2, cols, k3, q3, vb, gates, bias, wkv, wqg, marks, outs, ss, rs,
+    xp, wp, small, plane0, plane1, after, mid, mid2, cols, k3, q3, vb, gates, bias, wkv, wqg, w_out3, marks, outs, ss, rs,
 ):
-    r, q = lax.axis_index("row"), lax.axis_index("head")
+    r, head = lax.axis_index("row"), lax.axis_index("head")
     z, s = r // 8, lax.rem(r, 8)
     y, xh = s // 2, lax.rem(s, 2)
-    core, xlo = lax.rem(q, 2), q // 2
+    core, xlo = lax.rem(head, 2), head // 2
     other_core = (r, xlo * 2 + 1 - core)
     other_x = (r, (1 - xlo) * 2 + core)
-    q_core, q_x = other_core[1], other_x[1]
-    q_far = (1 - xlo) * 2 + 1 - core
+    head_core, head_x, head_far = other_core[1], other_x[1], (1 - xlo) * 2 + 1 - core
+    side = lax.rem(xlo + xh, 2)
+    q, q_core = side * 2 + core, side * 2 + 1 - core
+    q_x, q_far = (1 - side) * 2 + core, (1 - side) * 2 + 1 - core
+
+    def twin(there):
+        other = lax.rem(lax.rem(there, 2) + xh, 2)
+        return (z * 8 + there, lax.rem(xlo + other, 2) * 2 + core)
 
     def at_z(k):
-        return (lax.rem(z + k, 16) * 8 + s, q)
+        return (lax.rem(z + k, 16) * 8 + s, head)
 
     def at_y(k):
-        return (z * 8 + lax.rem(y + k, 4) * 2 + xh, q)
+        return (z * 8 + lax.rem(y + k, 4) * 2 + xh, head)
 
     def at_s(k):
-        return (z * 8 + lax.rem(s + k, 8), q)
-
-    at_x = (z * 8 + y * 2 + 1 - xh, q)
+        return twin(lax.rem(s + k, 8))
+
+    at_x = twin(y * 2 + 1 - xh)
 
     def send(src, dst, left, slot, device):
         pltpu.make_async_remote_copy(
@@ -109,7 +115,7 @@
         pltpu.make_async_copy(shift_in, ln_shift, rs.at[LOCAL + 2]),
         pltpu.make_async_copy(wb_in, wb_own, rs.at[LOCAL + 3]),
         pltpu.make_async_copy(cb_in, cb_own, rs.at[LOCAL + 4]),
-        pltpu.make_async_copy(w_own, wp.at[q], rs.at[LOCAL + 5]),
+        pltpu.make_async_copy(w_own, wp.at[head], rs.at[LOCAL + 5]),
         pltpu.make_async_copy(mask_in, mask, rs.at[LOCAL + 6]),
         pltpu.make_async_copy(chain_in, chain, rs.at[LOCAL + 7]),
         pltpu.make_async_copy(w_out_in, w_out, rs.at[LOCAL + 8]),
@@ -127,14 +133,14 @@
     def greet(device):
         pl.semaphore_signal(barrier, inc=1, device_id=device, device_id_type=MESH)
 
-    loop(1, 4, lambda k: greet((r, lax.rem(q + k, 4))))
+    loop(1, 4, lambda k: greet((r, lax.rem(head + k, 4))))
     loop(0, 15, lambda i: greet(at_z(far_first(i))))
     loop(1, 8, lambda k: greet(at_s(k)))
     for copy in local[6:]:
         copy.start()
     for copy in local[:6]:
         copy.wait()
-    small[q] = jnp.concatenate(
+    small[head] = jnp.concatenate(
         [
             wb_own[...],
             jnp.broadcast_to(cb_own[0:1, 0:1], (1, 128)),
@@ -145,9 +151,9 @@
     )
     pl.semaphore_wait(barrier, 25)
 
-    loop(1, 4, lambda k: send(small.at[q], small.at[q], LEFT_SMALL, SMALL, (r, lax.rem(q + k, 4))))
-    send(wp.at[q], wp.at[q], LEFT_W, W_X, other_x)
-    send(wp.at[q], wp.at[q], LEFT_W, W_CORE, other_core)
+    loop(1, 4, lambda k: send(small.at[head], small.at[head], LEFT_SMALL, SMALL, (r, lax.rem(head + k, 4))))
+    send(wp.at[head], wp.at[head], LEFT_W, W_X, other_x)
+    send(wp.at[head], wp.at[head], LEFT_W, W_CORE, other_core)
 
     own_normed = jnp.concatenate(
         [normalize(pair[q, pl.ds(t, 128, stride=4), :], ln_gain[0:1], ln_shift[0:1]) for t in range(4)], axis=0
@@ -216,8 +222,8 @@
     both = pl.ds(0, 16)
     gather_z(0, 0, both)
 
-    arrived(wp.at[q_x], W_X)
-    send(wp.at[q_x], wp.at[q_x], LEFT_W, W_FWD, other_core)
+    arrived(wp.at[head_x], W_X)
+    send(wp.at[head_x], wp.at[head_x], LEFT_W, W_FWD, other_core)
 
     for copy in local[6:]:
         copy.wait()
@@ -228,10 +234,12 @@
     place = lax.broadcasted_iota(jnp.int32, (512, 128), 0) // 4 == lax.broadcasted_iota(jnp.int32, (512, 128), 1)
     marks[...] = dot(value, place.astype(F32), ((1,), (0,)), highest)
 
-    arrived(wp.at[q_core], W_CORE)
-    arrived(wp.at[q_far], W_FWD)
+    arrived(wp.at[head_core], W_CORE)
+    arrived(wp.at[head_far], W_FWD)
 
     def weights(layer):
+        out_high, out_low = split(w_out[layer])
+        w_out3[layer] = jnp.concatenate([out_high, out_high, out_low], axis=0)
         for h in range(4):
             turned = wp[h, layer].T
             for ref, rows in ((wkv, turned[32:96]), (wqg, jnp.concatenate([turned[0:32], turned[96:128]], axis=0))):
@@ -271,15 +279,18 @@
                 bias[h, :, 128 * t : 128 * t + 128] = tile + small[h, 2 + layer : 3 + layer, :] * same + key_bias
 
     def attend(a, layer):
-        heads = []
-        for h in range(4):
-            score = dot(q3[a, h], k3[a, h], ((0,), (0,))) + bias[h]
-            weight = jnp.exp(score - jnp.max(score, axis=-1, keepdims=True))
-            weight_high, weight_low = split(weight)
-            total = dot(vb[a, h], weight_high, ((1,), (1,))) + dot(vb[a, h], weight_low, ((1,), (1,)))
-            heads.append((total[0:32] + total[32:64]) / total[64:65] * gates[a, pl.ds(32 * h, 32), :])
-        joined = jnp.concatenate(heads, axis=0)
-        return xp[a, q] + dot(joined, w_out[layer], ((0,), (0,)), highest)
+        four = range(4)
+        scores = [dot(q3[a, h], k3[a, h], ((0,), (0,))) + bias[h] for h in four]
+        tops = [jnp.max(scores[h], axis=-1, keepdims=True) for h in four]
+        weights = [split(jnp.exp(scores[h] - tops[h])) for h in four]
+        totals = [
+            (dot(weights[h][0], vb[a, h], ((1,), (1,))) + dot(weights[h][1], vb[a, h], ((1,), (1,)))).T for h in four
+        ]
+        heads = [
+            (totals[h][0:32] + totals[h][32:64]) / totals[h][64:65] * gates[a, pl.ds(32 * h, 32), :] for h in four
+        ]
+        high, low = split(jnp.concatenate(heads, axis=0))
+        return xp[a, q] + dot(jnp.concatenate([high, low, high], axis=0), w_out3[layer], ((0,), (0,)))
 
     weights(0)
 
@@ -467,6 +478,7 @@
             pltpu.VMEM((4, 128, 512), F32),
             pltpu.VMEM((256, 256), BF16),
             pltpu.VMEM((256, 256), BF16),
+            pltpu.VMEM((2, 384, 128), BF16),
             pltpu.VMEM((8, 128), F32),
             pltpu.VMEM((4, 4, 128, 128), F32),
             pltpu.SemaphoreType.DMA((leave.count,)),

time: 89.4 us -> 84.3 us (0.943)
  Pallas kernels: 88.3 us -> 83.2 us
    pallas_call x1, Pallas kernels: 88.3 us -> 83.2 us  [shards(): pl.pallas_call(kernel, out_shape=jax.ShapeDtypeStruct((2048, 128), F32),...]
where the time goes in v3:
time: 84.3 us; the launch traced here: 84.1 us
  Pallas kernels  83.2 us (99%)
  local copies, waits for them, and re-layouts  0.97 us (1%)
    pallas_call x1, Pallas kernels, shards(): pl.pallas_call(kernel, out_shape=jax.ShapeDtypeStruct((2048, 128), F32),...  83.2 us

profile of v3, /device:TPU:1, one launch (start us, length us, event | category | flops | bytes accessed | tf_op | source)
XLA Modules:
  0.0 84.1 jit_solution(9391083615652039085)
XLA Ops:
  0.0 83.2 %shard_map.91 = f32[2048,128]{1,0:T(8,128)S(1)} custom-call(f32[4,512,128]{2,1,0:T(8,128)} %pair_in.1, s32[1,512]{1,0:T(1,128)} %bitcast.8, s32[1,512]{1,0:T(1,128)} %bitcast.9, f32[2,128]{1,0:T(2,128)} %gain_in.1, f32[2,128]{1,0:T(2,128)} %shift_in.1, f32[2,128,128]{2,1,0:T(8,128)} %bitcast.7, f32[2,128]{1,0:T(2,128)} %bitcast.10, f32[1,2]{1,0:T(1,128)} %bitcast.11, ...), custom_call_target="tpu_custom_call" | custom-call | tf_op jit(solution)/shard_map/pallas_call | solution.py:451
  83.2 1.0 %copy.11 = f32[512,4,128]{2,1,0:T(4,128)} copy(f32[512,4,128]{2,1,0:T(4,128)S(1)} %bitcast.6) | data formatting | bytes 2097152

commit v4 on v3

--- a/solution.py
+++ b/solution.py
@@ -234,6 +234,9 @@
     place = lax.broadcasted_iota(jnp.int32, (512, 128), 0) // 4 == lax.broadcasted_iota(jnp.int32, (512, 128), 1)
     marks[...] = dot(value, place.astype(F32), ((1,), (0,)), highest)
 
+    gather_z_wait(0, 0, both, 0)
+    start_yx(0, 0)
+    start_xy(0, 0)
     arrived(wp.at[head_core], W_CORE)
     arrived(wp.at[head_far], W_FWD)
 
@@ -295,9 +298,12 @@
     weights(0)
 
     def first_project(a):
-        gather_z_wait(0, 0, both, a)
-        start_yx(0, a)
-        start_xy(0, a)
+        @pl.when(a > 0)
+        def _():
+            gather_z_wait(0, 0, both, a)
+            start_yx(0, a)
+            start_xy(0, a)
+
         for t in range(4):
             xp[a, t] = pair[a, pl.ds(t, 128, stride=4), :]
         project(a, 0)
@@ -317,12 +323,9 @@
         row = attend(a, 0)
         after[a] = row
 
-        def leave_z(i):
-            k = far_first(i)
+        for k in (8, 9, 7, 10, 6, 11, 5, 12, 4, 13, 3, 14, 2, 15, 1):
             rows = pl.ds(pl.multiple_of(lax.rem(z + k, 16) * 8, 8), 8)
             send(after.at[a, rows], mid.at[a, z], LEFT_PAIR_Z, PAIR_Z + a, at_z(k))
-
-        loop(0, 15, leave_z)
         mid[a, z] = after[a, pl.ds(pl.multiple_of(z * 8, 8), 8), :]
         normed = normalize(row, ln_gain[1:2], ln_shift[1:2])
         mine = dot(small[...].reshape(32, 128), normed, ((1,), (1,)), highest)
@@ -421,12 +424,8 @@
         send(block, block, LEFT_OUT, OUT_CORE + c, other_core)
         out[pl.ds(4 * q + c, 128, stride=16), :] = result
 
-        @pl.when(c > 1)
-        def _():
-            out_pass_on(c - 2)
-
     loop(0, 4, second_attend)
-    loop(2, 4, out_pass_on)
+    loop(0, 4, out_pass_on)
 
     def out_end(c):
         arrived(outs.at[c, q_far], OUT_FWD + c)

time: 84.3 us -> 83.2 us (0.987)
  Pallas kernels: 83.2 us -> 82.1 us
    pallas_call x1, Pallas kernels: 83.2 us -> 82.1 us  [shards(): pl.pallas_call(kernel, out_shape=jax.ShapeDtypeStruct((2048, 128), F32),...]
where the time goes in v4:
time: 83.2 us; the launch traced here: 83.1 us
  Pallas kernels  82.1 us (99%)
  local copies, waits for them, and re-layouts  0.97 us (1%)
    pallas_call x1, Pallas kernels, shards(): pl.pallas_call(kernel, out_shape=jax.ShapeDtypeStruct((2048, 128), F32),...  82.1 us

profile of v4, /device:TPU:1, one launch (start us, length us, event | category | flops | bytes accessed | tf_op | source)
XLA Modules:
  0.0 83.1 jit_solution(9435465326361699496)
XLA Ops:
  0.0 82.1 %shard_map.91 = f32[2048,128]{1,0:T(8,128)S(1)} custom-call(f32[4,512,128]{2,1,0:T(8,128)} %pair_in.1, s32[1,512]{1,0:T(1,128)} %bitcast.8, s32[1,512]{1,0:T(1,128)} %bitcast.9, f32[2,128]{1,0:T(2,128)} %gain_in.1, f32[2,128]{1,0:T(2,128)} %shift_in.1, f32[2,128,128]{2,1,0:T(8,128)} %bitcast.7, f32[2,128]{1,0:T(2,128)} %bitcast.10, f32[1,2]{1,0:T(1,128)} %bitcast.11, ...), custom_call_target="tpu_custom_call" | custom-call | tf_op jit(solution)/shard_map/pallas_call | solution.py:450
  82.1 1.0 %copy.11 = f32[512,4,128]{2,1,0:T(4,128)} copy(f32[512,4,128]{2,1,0:T(4,128)S(1)} %bitcast.6) | data formatting | bytes 2097152
